TPU v7x, 32 devices: a whole 2x2x4 slice. The times are simulated.
32 devices in a mesh: row: 8 (over y, x, core), col: 4 (over z).
Axes of the slice: x: 2, y: 2, z: 4, core: 2. Of those that a mesh axis runs over, the one named last changes fastest.
Arguments:
- features: bfloat16 [16384, 1024], P(('row', 'col')), may hold values from 0 to 4, as said below
- coords: float32 [64, 16384], P(None, ('row', 'col')), may hold values from -1 to 1
Outputs:
- placed: float32 [64, 16384], P(None, ('row', 'col'))
- row_stress: float32 [16384], P(('row', 'col'))
- stress_norm: float32 [], replicated
Inputs may be any that keep to these rules, and one draw needn't show every extreme that they name: `features`: every molecule has at least one nonzero feature.
All inputs are finite; a program needn't handle non-finite values.
Results may differ from a plain program's by a relative error of at most 0.0003.
Values may be sent and summed in bfloat16 or wider, within the bound.
A program may use at most 192 MiB of HBM per device.

v0:
```python
import jax
import jax.numpy as jnp
from jax import lax
from jax.sharding import PartitionSpec as P

ITERS = 2
FLOOR = 0.25
EXACT = lax.Precision.HIGHEST


def from_root(block, axis, owner):
    block = jnp.where(lax.axis_index(axis) == owner, block, jnp.zeros_like(block))
    return lax.psum(block, axis)


def squares_of(values):
    return jnp.einsum("rf,rf->r", values, values, preferred_element_type=jnp.float32)


def tanimoto(left_rows, left_sq, right_rows):
    right_sq = squares_of(right_rows)
    common = lax.dot_general(
        left_rows, right_rows, (((1,), (1,)), ((), ())), preferred_element_type=jnp.float32
    )
    return 1.0 - common / (left_sq[:, None] + right_sq[None, :] - common)


def guttman_terms(dissim, x_rows, x_cols):
    coord_dim, row_len = x_rows.shape
    block_len = min(512, row_len)
    block_count = row_len // block_len
    col_norms = jnp.sum(x_cols * x_cols, axis=0)
    dis_blocks = dissim.reshape(block_count, block_len, dissim.shape[1])
    x_blocks = jnp.moveaxis(x_rows.reshape(coord_dim, block_count, block_len), 1, 0)

    def one_block(inputs):
        dis_blk, x_blk = inputs
        blk_norms = jnp.sum(x_blk * x_blk, axis=0)
        inner = lax.dot_general(
            x_blk,
            x_cols,
            (((0,), (0,)), ((), ())),
            precision=EXACT,
            preferred_element_type=jnp.float32,
        )
        distance = jnp.sqrt(
            jnp.maximum(blk_norms[:, None] + col_norms[None, :] - 2.0 * inner, FLOOR * FLOOR)
        )
        ratios = dis_blk / distance
        pulled = lax.dot_general(
            x_cols,
            ratios,
            (((1,), (1,)), ((), ())),
            precision=EXACT,
            preferred_element_type=jnp.float32,
        )
        pull_terms = x_blk * jnp.sum(ratios, axis=1)[None, :] - pulled
        stress = jnp.sum(jnp.square(dis_blk - distance), axis=1)
        return (pull_terms, stress)

    pull_terms, stress = lax.map(one_block, (dis_blocks, x_blocks))
    return (jnp.moveaxis(pull_terms, 0, 1).reshape(coord_dim, row_len), stress.reshape(row_len))


def on_device(features, coords):
    rows_n = lax.axis_size("row")
    cols_n = lax.axis_size("col")
    row_at = lax.axis_index("row")
    col_at = lax.axis_index("col")
    ratio_k = rows_n // cols_n
    share_len = coords.shape[1]
    row_len = share_len * cols_n
    molecules = row_len * rows_n
    feature_rows = lax.all_gather(features, "col", axis=0, tiled=True)
    rows_sq = squares_of(feature_rows)
    pieces = []
    for offset in range(ratio_k):
        feature_cols = from_root(feature_rows, "row", col_at * ratio_k + offset)
        pieces.append(tanimoto(feature_rows, rows_sq, feature_cols))
    dissim = jnp.concatenate(pieces, axis=1)
    dissim_sq = jnp.sum(dissim * dissim)
    current = coords
    row_stress = jnp.zeros((share_len,), jnp.float32)
    for sweep in range(ITERS):
        everything = lax.all_gather(current, ("row", "col"), axis=1, tiled=True)
        x_rows = lax.dynamic_slice_in_dim(everything, row_at * row_len, row_len, 1)
        x_cols = lax.dynamic_slice_in_dim(
            everything, col_at * row_len * ratio_k, row_len * ratio_k, 1
        )
        pull_terms, stress = guttman_terms(dissim, x_rows, x_cols)
        new_share, stress_share = (
            lax.psum_scatter(pull_terms, "col", scatter_dimension=1, tiled=True),
            lax.psum_scatter(stress, "col", scatter_dimension=0, tiled=True),
        )
        current = new_share / molecules
        row_stress = stress_share / molecules
    local_stress = jnp.sum(row_stress)
    stress_total, dissim_total = lax.psum((local_stress, dissim_sq), ("row", "col"))
    stress_norm = molecules * stress_total / dissim_total
    return (current, row_stress, stress_norm)


def solution(mesh):
    return jax.shard_map(
        on_device,
        mesh=mesh,
        in_specs=(P(("row", "col"), None), P(None, ("row", "col"))),
        out_specs=(P(None, ("row", "col")), P(("row", "col")), P()),
        check_vma=False,
    )
```

profile of v0, /device:TPU:0, one launch (start us, length us, event | category | flops | bytes accessed | tf_op | source)
XLA Modules:
  0.0 698.3 jit_solution(13126097829784607838)
XLA Ops:
  8.7 84.4 %all-gather.6.cloned.1.call-done = bf16[2048,1024]{1,0:T(8,128)(2,1)} async-done(((bf16[512,1024]{1,0:T(8,128)(2,1)}), bf16[2048,1024]{1,0:T(8,128)(2,1)}) %all-gather.6.cloned.1.call-update) | async-done | bytes 4194320 | tf_op jit(solution)/shard_map/all_gather | solution.py:74
  102.2 54.3 %all-gather.4.cloned.1.call-done = f32[64,16384]{1,0:T(8,128)} async-done(((f32[64,512]{1,0:T(8,128)}), f32[64,16384]{1,0:T(8,128)}) %all-gather.4.cloned.1.call-update) | async-done | bytes 4194320 | tf_op jit(solution)/shard_map/all_gather | solution.py:85
  159.3 126.3 %all-reduce.5.cloned.1.call-done = (bf16[2048,1024]{1,0:T(8,128)(2,1)}, bf16[2048,1024]{1,0:T(8,128)(2,1)}) async-done(((bf16[2048,1024]{1,0:T(8,128)(2,1)}, bf16[2048,1024]{1,0:T(8,128)(2,1)}), (bf16[2048,1024]{1,0:T(8,128)(2,1)}, bf16[2048,1024]{1,0:T(8,128)(2,1)})) %all-reduce.5.cloned.1.call-update) | async-done | bytes 8388624 | tf_op jit(solution)/shard_map/psum | solution.py:13
  290.9 11.4 %fusion.9 = f32[2048,2048]{0,1:T(8,128)S(1)} fusion(bf16[2048,1024]{1,0:T(8,128)(2,1)} %get-tuple-element.146, bf16[2048,1024]{1,0:T(8,128)(2,1)S(1)} %copy-done, f32[2048]{0:T(1024)S(1)} %get-tuple-element.161, f32[2048]{0:T(1024)S(1)} %fusion.13), kind=kOutput, calls=%fused_computation.25 | convolution fusion | flops 8606711808 | bytes 25182208 | tf_op jit(solution)/shard_map/dot_general | solution.py:22
  302.3 14.4 %fusion.10 = f32[2048,2048]{0,1:T(8,128)} fusion(bf16[2048,1024]{1,0:T(8,128)(2,1)} %get-tuple-element.145, bf16[2048,1024]{1,0:T(8,128)(2,1)S(1)} %copy-done, f32[2048]{0:T(1024)S(1)} %get-tuple-element.160, f32[2048]{0:T(1024)S(1)} %fusion.13), kind=kOutput, calls=%fused_computation.26 | convolution fusion | flops 8606711808 | bytes 25182208 | tf_op jit(solution)/shard_map/dot_general | solution.py:22
  316.7 20.2 %multiply_reduce_fusion.2 = (f32[]{:T(128)}, f32[2048,4096]{0,1:T(8,128)}) fusion(f32[2048,2048]{0,1:T(8,128)} %fusion.10, f32[2048,2048]{0,1:T(8,128)S(1)} %fusion.9), kind=kLoop, calls=%fused_computation.22 | loop fusion | flops 25165824 | bytes 67108864 | tf_op jit(solution)/shard_map/reduce_sum | solution.py:81
  336.9 31.1 %copy.33 = f32[2048,4096]{1,0:T(8,128)} copy(f32[2048,4096]{0,1:T(8,128)} %get-tuple-element.157) | data formatting | bytes 67108864 | tf_op jit(solution)/shard_map/while | solution.py:61
  368.0 78.5 %while.22 = (s32[]{:T(128)}, f32[4,64,512]{2,1,0:T(8,128)S(1)}, f32[4,64,512]{2,0,1:T(4,128)S(1)}, f32[4,512,4096]{2,1,0:T(8,128)}, f32[4096]{0:T(1024)S(1)}, /*index=5*/f32[64,4096]{1,0:T(8,128)S(1)}, s32[]{:T(128)}) while((s32[]{:T(128)}, f32[4,64,512]{2,1,0:T(8,128)S(1)}, f32[4,64,512]{2,0,1:T(4,128)S(1)}, f32[4,512,4096]{2,1,0:T(8,128)}, ...), condition=%wide.region_6.7_spmd, body=%wide.region_3.6_spmd.sunk | while | flops 3233938432 | bytes 28074072 | solution.py:61
  368.4 11.1 %fusion.37 = (f32[512]{0:T(512)S(1)}, f32[512,4096]{1,0:T(8,128)S(1)}) fusion(f32[64,4096]{1,0:T(8,128)S(1)} %get-tuple-element.271, f32[1,64,512]{2,0,1:T(1,128)S(1)} %constant_dynamic-slice_fusion.10, f32[4096]{0:T(1024)S(1)} %get-tuple-element.270, f32[512]{0:T(512)S(1)} %multiply_reduce_fusion.7, f32[4,512,4096]{2,1,0:T(8,128)} %get-tuple-element.269, ...), kind=kOutput, calls=%fused_computation.45.clone.1 | convolution fusion | flops 1623195136 | bytes 17977348 | tf_op jit(solution)/shard_map/while/body/eval_jaxpr/dot_general | solution.py:39
  388.0 11.1 %fusion.37 = (f32[512]{0:T(512)S(1)}, f32[512,4096]{1,0:T(8,128)S(1)}) fusion(f32[64,4096]{1,0:T(8,128)S(1)} %get-tuple-element.271, f32[1,64,512]{2,0,1:T(1,128)S(1)} %constant_dynamic-slice_fusion.10, f32[4096]{0:T(1024)S(1)} %get-tuple-element.270, f32[512]{0:T(512)S(1)} %multiply_reduce_fusion.7, f32[4,512,4096]{2,1,0:T(8,128)} %get-tuple-element.269, ...), kind=kOutput, calls=%fused_computation.45.clone.1 | convolution fusion | flops 1623195136 | bytes 17977348 | tf_op jit(solution)/shard_map/while/body/eval_jaxpr/dot_general | solution.py:39
  407.5 11.1 %fusion.37 = (f32[512]{0:T(512)S(1)}, f32[512,4096]{1,0:T(8,128)S(1)}) fusion(f32[64,4096]{1,0:T(8,128)S(1)} %get-tuple-element.271, f32[1,64,512]{2,0,1:T(1,128)S(1)} %constant_dynamic-slice_fusion.10, f32[4096]{0:T(1024)S(1)} %get-tuple-element.270, f32[512]{0:T(512)S(1)} %multiply_reduce_fusion.7, f32[4,512,4096]{2,1,0:T(8,128)} %get-tuple-element.269, ...), kind=kOutput, calls=%fused_computation.45.clone.1 | convolution fusion | flops 1623195136 | bytes 17977348 | tf_op jit(solution)/shard_map/while/body/eval_jaxpr/dot_general | solution.py:39
  427.1 11.1 %fusion.37 = (f32[512]{0:T(512)S(1)}, f32[512,4096]{1,0:T(8,128)S(1)}) fusion(f32[64,4096]{1,0:T(8,128)S(1)} %get-tuple-element.271, f32[1,64,512]{2,0,1:T(1,128)S(1)} %constant_dynamic-slice_fusion.10, f32[4096]{0:T(1024)S(1)} %get-tuple-element.270, f32[512]{0:T(512)S(1)} %multiply_reduce_fusion.7, f32[4,512,4096]{2,1,0:T(8,128)} %get-tuple-element.269, ...), kind=kOutput, calls=%fused_computation.45.clone.1 | convolution fusion | flops 1623195136 | bytes 17977348 | tf_op jit(solution)/shard_map/while/body/eval_jaxpr/dot_general | solution.py:39
  447.4 21.9 %reduce-scatter.3.cloned.1.call-done = f32[64,512]{1,0:T(8,128)} async-done(((f32[64,2048]{1,0:T(8,128)}), f32[64,512]{1,0:T(8,128)}) %reduce-scatter.3.cloned.1.call-update) | async-done | bytes 131088 | tf_op jit(solution)/shard_map/reduce_scatter | solution.py:92
  471.0 62.4 %all-gather.8.cloned.1.call-done = f32[64,16384]{1,0:T(8,128)} async-done(((f32[64,512]{1,0:T(8,128)}), f32[64,16384]{1,0:T(8,128)}) %all-gather.8.cloned.1.call-update) | async-done | bytes 4194320 | tf_op jit(solution)/shard_map/all_gather | solution.py:85
  536.3 98.9 %while.23 = (s32[]{:T(128)}, f32[4,64,512]{2,1,0:T(8,128)S(1)}, f32[4,512]{1,0:T(4,128)S(1)}, f32[4,64,512]{2,0,1:T(4,128)S(1)}, f32[4,512,4096]{2,1,0:T(8,128)}...) while((s32[]{:T(128)}, f32[4,64,512]{2,1,0:T(8,128)S(1)}, ...), condition=%wide.region_13.14_spmd, body=%wide.region_9.13_spmd.sunk | while | flops 3242326528 | bytes 36469864 | solution.py:61
  536.7 13.9 %fusion.41 = (f32[512]{0:T(512)S(1)}, f32[512]{0:T(512)S(1)}, f32[512,4096]{1,0:T(8,128)S(1)}) fusion(f32[4,512,4096]{2,1,0:T(8,128)} %get-tuple-element.295, s32[]{:T(128)} %get-tuple-element.282, f32[64,4096]{1,0:T(8,128)S(1)} %get-tuple-element.297, f32[1,64,512]{2,0,1:T(1,128)S(1)} %constant_dynamic-slice_fusion.11, ...), kind=kOutput, calls=%fused_computation.11.clone.1 | convolution fusion | flops 1629486080 | bytes 17979396 | tf_op jit(solution)/shard_map/while/body/eval_jaxpr/dot_general | solution.py:39
  550.6 10.5 %fusion.42 = f32[4,64,512]{2,1,0:T(8,128)S(1)} fusion(f32[4,64,512]{2,1,0:T(8,128)S(1)} %get-tuple-element.283, s32[]{:T(128)} %get-tuple-element.282, f32[64,4096]{1,0:T(8,128)S(1)} %get-tuple-element.297, f32[1,64,512]{2,0,1:T(1,128)S(1)} %constant_dynamic-slice_fusion.11, f32[512]{0:T(512)S(1)} %get-tuple-element.249, ...), kind=kOutput, calls=%fused_computation.16.clone.1 | convolution fusion | flops 1612775424 | bytes 18091008 | tf_op jit(solution)/shard_map/while/body/eval_jaxpr/dot_general | solution.py:50
  561.4 13.9 %fusion.41 = (f32[512]{0:T(512)S(1)}, f32[512]{0:T(512)S(1)}, f32[512,4096]{1,0:T(8,128)S(1)}) fusion(f32[4,512,4096]{2,1,0:T(8,128)} %get-tuple-element.295, s32[]{:T(128)} %get-tuple-element.282, f32[64,4096]{1,0:T(8,128)S(1)} %get-tuple-element.297, f32[1,64,512]{2,0,1:T(1,128)S(1)} %constant_dynamic-slice_fusion.11, ...), kind=kOutput, calls=%fused_computation.11.clone.1 | convolution fusion | flops 1629486080 | bytes 17979396 | tf_op jit(solution)/shard_map/while/body/eval_jaxpr/dot_general | solution.py:39
  586.0 13.9 %fusion.41 = (f32[512]{0:T(512)S(1)}, f32[512]{0:T(512)S(1)}, f32[512,4096]{1,0:T(8,128)S(1)}) fusion(f32[4,512,4096]{2,1,0:T(8,128)} %get-tuple-element.295, s32[]{:T(128)} %get-tuple-element.282, f32[64,4096]{1,0:T(8,128)S(1)} %get-tuple-element.297, f32[1,64,512]{2,0,1:T(1,128)S(1)} %constant_dynamic-slice_fusion.11, ...), kind=kOutput, calls=%fused_computation.11.clone.1 | convolution fusion | flops 1629486080 | bytes 17979396 | tf_op jit(solution)/shard_map/while/body/eval_jaxpr/dot_general | solution.py:39
  599.9 10.5 %fusion.42 = f32[4,64,512]{2,1,0:T(8,128)S(1)} fusion(f32[4,64,512]{2,1,0:T(8,128)S(1)} %get-tuple-element.283, s32[]{:T(128)} %get-tuple-element.282, f32[64,4096]{1,0:T(8,128)S(1)} %get-tuple-element.297, f32[1,64,512]{2,0,1:T(1,128)S(1)} %constant_dynamic-slice_fusion.11, f32[512]{0:T(512)S(1)} %get-tuple-element.249, ...), kind=kOutput, calls=%fused_computation.16.clone.1 | convolution fusion | flops 1612775424 | bytes 18091008 | tf_op jit(solution)/shard_map/while/body/eval_jaxpr/dot_general | solution.py:50
  610.7 13.9 %fusion.41 = (f32[512]{0:T(512)S(1)}, f32[512]{0:T(512)S(1)}, f32[512,4096]{1,0:T(8,128)S(1)}) fusion(f32[4,512,4096]{2,1,0:T(8,128)} %get-tuple-element.295, s32[]{:T(128)} %get-tuple-element.282, f32[64,4096]{1,0:T(8,128)S(1)} %get-tuple-element.297, f32[1,64,512]{2,0,1:T(1,128)S(1)} %constant_dynamic-slice_fusion.11, ...), kind=kOutput, calls=%fused_computation.11.clone.1 | convolution fusion | flops 1629486080 | bytes 17979396 | tf_op jit(solution)/shard_map/while/body/eval_jaxpr/dot_general | solution.py:39
  624.6 10.5 %fusion.42 = f32[4,64,512]{2,1,0:T(8,128)S(1)} fusion(f32[4,64,512]{2,1,0:T(8,128)S(1)} %get-tuple-element.283, s32[]{:T(128)} %get-tuple-element.282, f32[64,4096]{1,0:T(8,128)S(1)} %get-tuple-element.297, f32[1,64,512]{2,0,1:T(1,128)S(1)} %constant_dynamic-slice_fusion.11, f32[512]{0:T(512)S(1)} %get-tuple-element.249, ...), kind=kOutput, calls=%fused_computation.16.clone.1 | convolution fusion | flops 1612775424 | bytes 18091008 | tf_op jit(solution)/shard_map/while/body/eval_jaxpr/dot_general | solution.py:50
  637.3 10.5 %all-reduce = f32[2048]{0:T(1024)S(1)} all-reduce(f32[2048]{0:T(1024)S(1)} %bitcast.124), channel_id=4, replica_groups=mesh['row'=8,'col'=4] {'col'}, use_global_device_ids=true, to_apply=%region_15.16.clone | all-reduce | flops 2048 | bytes 16384
  649.1 38.3 %all-reduce.1 = (f32[]{:T(128)}, f32[]{:T(128)}) all-reduce(f32[]{:T(128)} %get-tuple-element.147, f32[]{:T(128)} %get-tuple-element.156), channel_id=1, replica_groups=mesh['row'=8,'col'=4] {'row','col'}, use_global_device_ids=true, to_apply=%region_17.18 | all-reduce | flops 2 | bytes 16 | tf_op jit(solution)/shard_map/psum | solution.py:98
  (61 shorter events, 73.2 us)
Async XLA Ops:
  7.2 85.9 %all-gather.6.cloned.1.call-start = ((), (), s32[]{:S(2)}) async-start(), calls=%async_computation.3 | async-start | bytes 5242880 | tf_op jit(solution)/shard_map/all_gather | solution.py:74
  7.9 148.6 %all-gather.4.cloned.1.call-start = ((), (), s32[]{:S(2)}) async-start(), calls=%async_computation.2 | async-start | bytes 4325376 | tf_op jit(solution)/shard_map/all_gather | solution.py:85
  8.6 276.9 %all-reduce.5.cloned.1.call-start = ((), (), s32[]{:S(2)}) async-start(), calls=%async_computation.7 | async-start | bytes 16777216 | tf_op jit(solution)/shard_map/psum | solution.py:13
  99.0 370.3 %reduce-scatter.3.cloned.1.call-start = ((), (), s32[]{:S(2)}) async-start(), calls=%async_computation.4 | async-start | bytes 655360 | tf_op jit(solution)/shard_map/reduce_scatter | solution.py:92
  285.5 5.3 copy-start
  447.4 86.0 %all-gather.8.cloned.1.call-start = ((), (), s32[]{:S(2)}) async-start(), calls=%async_computation.5 | async-start | bytes 4325376 | tf_op jit(solution)/shard_map/all_gather | solution.py:85
  470.9 217.8 %reduce-scatter.5.cloned.1.call-start = ((), (), s32[]{:S(2)}) async-start(), calls=%async_computation.6 | async-start | bytes 655360 | tf_op jit(solution)/shard_map/reduce_scatter | solution.py:92
  536.3 99.8 %copy-start.1 = (u32[32]{0:T(128)S(1)}, u32[32]{0:T(128)}, u32[]{:S(2)}) copy-start(u32[32]{0:T(128)} %constant.75) | copy-start | bytes 388
Sparse Core Ops, SparseCore 0:
  9.6 83.4 all-gather.5
  96.1 60.2 all-gather.3
  160.2 125.3 all-reduce.4
  447.5 21.7 reduce-scatter.2
  473.3 60.0 all-gather.7
  636.2 19.9 reduce-scatter.4
where the time goes:
time: 699 us; the launch traced here: 698 us
  waiting for transfers between devices  351 us (50%)
  matrix products  201 us (29%)
  blocking collectives  48.8 us (7%)
  other arithmetic  41.9 us (6%)
  local copies, waits for them, and re-layouts  37.5 us (5%)
  between operations  17.4 us (2%)
    psum x1, waiting for transfers between devices, from_root(): return lax.psum(block, axis)  126 us
    all_gather x2, waiting for transfers between devices, on_device(): everything = lax.all_gather(current, ('row', 'col'), axis=1, tiled=True)  117 us
    dot_general x8, matrix products, one_block(): lax.dot_general(x_blk, x_cols, (((0,), (0,)), ((), ())), precision=EXACT,...  100 us
    all_gather x1, waiting for transfers between devices, on_device(): feature_rows = lax.all_gather(features, 'col', axis=0, tiled=True)  84.4 us
    dot_general x8, matrix products, one_block(): lax.dot_general(x_cols, ratios, (((1,), (1,)), ((), ())), precision=EXACT...  74.9 us
    psum x1, blocking collectives, on_device(): lax.psum((local_stress, dissim_sq), ('row', 'col'))  38.3 us
    while x1, local copies, waits for them, and re-layouts, guttman_terms(): pull_terms, stress = lax.map(one_block, (dis_blocks, x_blocks))  31.1 us
    dot_general x2, matrix products, tanimoto(): lax.dot_general(left_rows, right_rows, (((1,), (1,)), ((), ())), preferre...  25.8 us
  transfers between devices with their start and end apart: 6, of which 5 were waited for; matrix products, arithmetic and copies ran while one was open for 2% of the time, Pallas kernels for 0%

commit v1 on v0

--- a/solution.py
+++ b/solution.py
@@ -71,7 +71,12 @@
     share_len = coords.shape[1]
     row_len = share_len * cols_n
     molecules = row_len * rows_n
-    feature_rows = lax.all_gather(features, "col", axis=0, tiled=True)
+    ring = [features]
+    for hop in range(3):
+        ring.append(lax.ppermute(ring[-1], "col", [(dev, (dev + 1) % 4) for dev in range(4)]))
+    feature_rows = jnp.roll(
+        jnp.concatenate(ring[::-1], axis=0), (lax.axis_index("col") + 1) * ring[0].shape[0], axis=0
+    )
     rows_sq = squares_of(feature_rows)
     pieces = []
     for offset in range(ratio_k):

time: 699 us -> 652 us (0.933)
  waiting for transfers between devices: 351 us -> 285 us
  local copies, waits for them, and re-layouts: 37.5 us -> 44.9 us
    all_gather x1 -> x0, waiting for transfers between devices: 84.4 us -> none  [on_device(): feature_rows = lax.all_gather(features, 'col', axis=0, tiled=True)]
    ppermute x0 -> x3, waiting for transfers between devices: none -> 76.9 us  [on_device(): lax.ppermute(ring[-1], 'col', [(dev, (dev + 1) % 4) for dev in range(4)])]
    all_gather x2, waiting for transfers between devices: 117 us -> 60.2 us  [on_device(): everything = lax.all_gather(current, ('row', 'col'), axis=1, tiled=True)]
    unnamed x6 -> x19, local copies, waits for them, and re-layouts: 0.6 us -> 7.99 us
  transfers between devices with their start and end apart: 6 -> 8, of which waited for: 5 -> 6; matrix products, arithmetic and copies ran while one was open for 2% -> 14% of each run, Pallas kernels for 0% -> 0%
where the time goes in v1:
time: 652 us; the launch traced here: 646 us
  waiting for transfers between devices  285 us (44%)
  matrix products  204 us (31%)
  blocking collectives  48.9 us (8%)
  local copies, waits for them, and re-layouts  44.9 us (7%)
  other arithmetic  41.1 us (6%)
  between operations  18.8 us (3%)
    psum x1, waiting for transfers between devices, from_root(): return lax.psum(block, axis)  126 us
    dot_general x8, matrix products, one_block(): lax.dot_general(x_blk, x_cols, (((0,), (0,)), ((), ())), precision=EXACT,...  100 us
    ppermute x3, waiting for transfers between devices, on_device(): lax.ppermute(ring[-1], 'col', [(dev, (dev + 1) % 4) for dev in range(4)])  76.9 us
    dot_general x8, matrix products, one_block(): lax.dot_general(x_cols, ratios, (((1,), (1,)), ((), ())), precision=EXACT...  74.9 us
    all_gather x2, waiting for transfers between devices, on_device(): everything = lax.all_gather(current, ('row', 'col'), axis=1, tiled=True)  60.2 us
    psum x1, blocking collectives, on_device(): lax.psum((local_stress, dissim_sq), ('row', 'col'))  38 us
    while x1, local copies, waits for them, and re-layouts, guttman_terms(): pull_terms, stress = lax.map(one_block, (dis_blocks, x_blocks))  31.1 us
    dot_general x2, matrix products, tanimoto(): lax.dot_general(left_rows, right_rows, (((1,), (1,)), ((), ())), preferre...  28.3 us
  transfers between devices with their start and end apart: 8, of which 6 were waited for; matrix products, arithmetic and copies ran while one was open for 14% of the time, Pallas kernels for 0%

profile of v1, /device:TPU:0, one launch (start us, length us, event | category | flops | bytes accessed | tf_op | source)
XLA Modules:
  0.0 646.5 jit_solution(11102121443519563279)
XLA Ops:
  11.1 25.4 %collective-permute-done = bf16[512,1024]{1,0:T(8,128)(2,1)S(1)} collective-permute-done((bf16[512,1024]{1,0:T(8,128)(2,1)}, bf16[512,1024]{1,0:T(8,128)(2,1)S(1)}, u32[]{:S(2)}, u32[]{:S(2)}) %collective-permute-start) | collective-permute-done | bytes 1048608 | tf_op jit(solution)/shard_map/ppermute | solution.py:76
  36.5 26.1 %collective-permute-done.1 = bf16[512,1024]{1,0:T(8,128)(2,1)S(1)} collective-permute-done((bf16[512,1024]{1,0:T(8,128)(2,1)S(1)}, bf16[512,1024]{1,0:T(8,128)(2,1)S(1)}, u32[]{:S(2)}, u32[]{:S(2)}) %collective-permute-start.1) | collective-permute-done | bytes 1048608 | tf_op jit(solution)/shard_map/ppermute | solution.py:76
  62.7 25.3 %collective-permute-done.2 = bf16[512,1024]{1,0:T(8,128)(2,1)} collective-permute-done((bf16[512,1024]{1,0:T(8,128)(2,1)S(1)}, bf16[512,1024]{1,0:T(8,128)(2,1)}, u32[]{:S(2)}, u32[]{:S(2)}) %collective-permute-start.2) | collective-permute-done | bytes 1048608 | tf_op jit(solution)/shard_map/ppermute | solution.py:76
  104.3 125.7 %all-reduce.5.cloned.1.call-done = (bf16[2048,1024]{1,0:T(8,128)(2,1)}, bf16[2048,1024]{1,0:T(8,128)(2,1)}) async-done(((bf16[2048,1024]{1,0:T(8,128)(2,1)}, bf16[2048,1024]{1,0:T(8,128)(2,1)}), (bf16[2048,1024]{1,0:T(8,128)(2,1)}, bf16[2048,1024]{1,0:T(8,128)(2,1)})) %all-reduce.5.cloned.1.call-update) | async-done | bytes 8388624 | tf_op jit(solution)/shard_map/psum | solution.py:13
  235.4 13.9 %fusion.9 = f32[2048,2048]{0,1:T(8,128)S(1)} fusion(f32[2048]{0:T(1024)S(1)} %get-tuple-element.161, f32[2048]{0:T(1024)S(1)} %fusion.13, bf16[2048,1024]{1,0:T(8,128)(2,1)} %get-tuple-element.146, bf16[4096,1024]{1,0:T(8,128)(2,1)} %copy-done, s32[]{:T(128)S(6)} %select_n.37), kind=kOutput, calls=%fused_computation.25 | convolution fusion | flops 8606711808 | bytes 25182212 | tf_op jit(solution)/shard_map/dot_general | solution.py:22
  249.3 14.4 %fusion.10 = f32[2048,2048]{0,1:T(8,128)} fusion(f32[2048]{0:T(1024)S(1)} %get-tuple-element.160, f32[2048]{0:T(1024)S(1)} %fusion.13, bf16[2048,1024]{1,0:T(8,128)(2,1)} %get-tuple-element.145, bf16[4096,1024]{1,0:T(8,128)(2,1)S(1)} %bitcast.112, s32[]{:T(128)S(6)} %select_n.37), kind=kOutput, calls=%fused_computation.26 | convolution fusion | flops 8606711808 | bytes 25182212 | tf_op jit(solution)/shard_map/dot_general | solution.py:22
  263.7 20.3 %multiply_reduce_fusion.2 = (f32[]{:T(128)}, f32[2048,4096]{0,1:T(8,128)}) fusion(f32[2048,2048]{0,1:T(8,128)} %fusion.10, f32[2048,2048]{0,1:T(8,128)S(1)} %fusion.9), kind=kLoop, calls=%fused_computation.22 | loop fusion | flops 25165824 | bytes 67108864 | tf_op jit(solution)/shard_map/reduce_sum | solution.py:86
  284.0 31.1 %copy.33 = f32[2048,4096]{1,0:T(8,128)} copy(f32[2048,4096]{0,1:T(8,128)} %get-tuple-element.157) | data formatting | bytes 67108864 | tf_op jit(solution)/shard_map/while | solution.py:61
  318.0 78.4 %while.22 = (s32[]{:T(128)}, f32[4,64,512]{2,1,0:T(8,128)S(1)}, f32[4,64,512]{2,0,1:T(4,128)S(1)}, f32[4,512,4096]{2,1,0:T(8,128)}, f32[4096]{0:T(1024)S(1)}, /*index=5*/f32[64,4096]{1,0:T(8,128)S(1)}, s32[]{:T(128)}) while((s32[]{:T(128)}, f32[4,64,512]{2,1,0:T(8,128)S(1)}, f32[4,64,512]{2,0,1:T(4,128)S(1)}, f32[4,512,4096]{2,1,0:T(8,128)}, ...), condition=%wide.region_6.7_spmd, body=%wide.region_3.6_spmd.sunk | while | flops 3233938432 | bytes 28074072 | solution.py:61
  318.3 11.2 %fusion.39 = (f32[512]{0:T(512)S(1)}, f32[512,4096]{1,0:T(8,128)S(1)}) fusion(f32[64,4096]{1,0:T(8,128)S(1)} %get-tuple-element.271, f32[1,64,512]{2,0,1:T(1,128)S(1)} %constant_dynamic-slice_fusion.10, f32[4096]{0:T(1024)S(1)} %get-tuple-element.270, f32[512]{0:T(512)S(1)} %multiply_reduce_fusion.7, f32[4,512,4096]{2,1,0:T(8,128)} %get-tuple-element.269, ...), kind=kOutput, calls=%fused_computation.57.clone.1 | convolution fusion | flops 1623195136 | bytes 17977348 | tf_op jit(solution)/shard_map/while/body/eval_jaxpr/dot_general | solution.py:39
  337.9 11.1 %fusion.39 = (f32[512]{0:T(512)S(1)}, f32[512,4096]{1,0:T(8,128)S(1)}) fusion(f32[64,4096]{1,0:T(8,128)S(1)} %get-tuple-element.271, f32[1,64,512]{2,0,1:T(1,128)S(1)} %constant_dynamic-slice_fusion.10, f32[4096]{0:T(1024)S(1)} %get-tuple-element.270, f32[512]{0:T(512)S(1)} %multiply_reduce_fusion.7, f32[4,512,4096]{2,1,0:T(8,128)} %get-tuple-element.269, ...), kind=kOutput, calls=%fused_computation.57.clone.1 | convolution fusion | flops 1623195136 | bytes 17977348 | tf_op jit(solution)/shard_map/while/body/eval_jaxpr/dot_general | solution.py:39
  357.4 11.1 %fusion.39 = (f32[512]{0:T(512)S(1)}, f32[512,4096]{1,0:T(8,128)S(1)}) fusion(f32[64,4096]{1,0:T(8,128)S(1)} %get-tuple-element.271, f32[1,64,512]{2,0,1:T(1,128)S(1)} %constant_dynamic-slice_fusion.10, f32[4096]{0:T(1024)S(1)} %get-tuple-element.270, f32[512]{0:T(512)S(1)} %multiply_reduce_fusion.7, f32[4,512,4096]{2,1,0:T(8,128)} %get-tuple-element.269, ...), kind=kOutput, calls=%fused_computation.57.clone.1 | convolution fusion | flops 1623195136 | bytes 17977348 | tf_op jit(solution)/shard_map/while/body/eval_jaxpr/dot_general | solution.py:39
  377.0 11.1 %fusion.39 = (f32[512]{0:T(512)S(1)}, f32[512,4096]{1,0:T(8,128)S(1)}) fusion(f32[64,4096]{1,0:T(8,128)S(1)} %get-tuple-element.271, f32[1,64,512]{2,0,1:T(1,128)S(1)} %constant_dynamic-slice_fusion.10, f32[4096]{0:T(1024)S(1)} %get-tuple-element.270, f32[512]{0:T(512)S(1)} %multiply_reduce_fusion.7, f32[4,512,4096]{2,1,0:T(8,128)} %get-tuple-element.269, ...), kind=kOutput, calls=%fused_computation.57.clone.1 | convolution fusion | flops 1623195136 | bytes 17977348 | tf_op jit(solution)/shard_map/while/body/eval_jaxpr/dot_general | solution.py:39
  397.3 21.9 %reduce-scatter.3.cloned.1.call-done = f32[64,512]{1,0:T(8,128)} async-done(((f32[64,2048]{1,0:T(8,128)}), f32[64,512]{1,0:T(8,128)}) %reduce-scatter.3.cloned.1.call-update) | async-done | bytes 131088 | tf_op jit(solution)/shard_map/reduce_scatter | solution.py:97
  420.9 60.2 %all-gather.5.cloned.1.call-done = f32[64,16384]{1,0:T(8,128)} async-done(((f32[64,512]{1,0:T(8,128)}), f32[64,16384]{1,0:T(8,128)}) %all-gather.5.cloned.1.call-update) | async-done | bytes 4194320 | tf_op jit(solution)/shard_map/all_gather | solution.py:90
  484.0 98.8 %while.23 = (s32[]{:T(128)}, f32[4,64,512]{2,1,0:T(8,128)S(1)}, f32[4,512]{1,0:T(4,128)S(1)}, f32[4,64,512]{2,0,1:T(4,128)S(1)}, f32[4,512,4096]{2,1,0:T(8,128)}...) while((s32[]{:T(128)}, f32[4,64,512]{2,1,0:T(8,128)S(1)}, ...), condition=%wide.region_13.14_spmd, body=%wide.region_9.13_spmd.sunk | while | flops 3242326528 | bytes 36469864 | solution.py:61
  484.4 13.9 %fusion.43 = (f32[512]{0:T(512)S(1)}, f32[512]{0:T(512)S(1)}, f32[512,4096]{1,0:T(8,128)S(1)}) fusion(f32[4,512,4096]{2,1,0:T(8,128)} %get-tuple-element.295, s32[]{:T(128)} %get-tuple-element.282, f32[64,4096]{1,0:T(8,128)S(1)} %get-tuple-element.297, f32[1,64,512]{2,0,1:T(1,128)S(1)} %constant_dynamic-slice_fusion.11, ...), kind=kOutput, calls=%fused_computation.11.clone.1 | convolution fusion | flops 1629486080 | bytes 17979396 | tf_op jit(solution)/shard_map/while/body/eval_jaxpr/dot_general | solution.py:39
  498.3 10.5 %fusion.44 = f32[4,64,512]{2,1,0:T(8,128)S(1)} fusion(f32[4,64,512]{2,1,0:T(8,128)S(1)} %get-tuple-element.283, s32[]{:T(128)} %get-tuple-element.282, f32[64,4096]{1,0:T(8,128)S(1)} %get-tuple-element.297, f32[1,64,512]{2,0,1:T(1,128)S(1)} %constant_dynamic-slice_fusion.11, f32[512]{0:T(512)S(1)} %get-tuple-element.249, ...), kind=kOutput, calls=%fused_computation.16.clone.1 | convolution fusion | flops 1612775424 | bytes 18091008 | tf_op jit(solution)/shard_map/while/body/eval_jaxpr/dot_general | solution.py:50
  509.0 13.9 %fusion.43 = (f32[512]{0:T(512)S(1)}, f32[512]{0:T(512)S(1)}, f32[512,4096]{1,0:T(8,128)S(1)}) fusion(f32[4,512,4096]{2,1,0:T(8,128)} %get-tuple-element.295, s32[]{:T(128)} %get-tuple-element.282, f32[64,4096]{1,0:T(8,128)S(1)} %get-tuple-element.297, f32[1,64,512]{2,0,1:T(1,128)S(1)} %constant_dynamic-slice_fusion.11, ...), kind=kOutput, calls=%fused_computation.11.clone.1 | convolution fusion | flops 1629486080 | bytes 17979396 | tf_op jit(solution)/shard_map/while/body/eval_jaxpr/dot_general | solution.py:39
  533.7 13.9 %fusion.43 = (f32[512]{0:T(512)S(1)}, f32[512]{0:T(512)S(1)}, f32[512,4096]{1,0:T(8,128)S(1)}) fusion(f32[4,512,4096]{2,1,0:T(8,128)} %get-tuple-element.295, s32[]{:T(128)} %get-tuple-element.282, f32[64,4096]{1,0:T(8,128)S(1)} %get-tuple-element.297, f32[1,64,512]{2,0,1:T(1,128)S(1)} %constant_dynamic-slice_fusion.11, ...), kind=kOutput, calls=%fused_computation.11.clone.1 | convolution fusion | flops 1629486080 | bytes 17979396 | tf_op jit(solution)/shard_map/while/body/eval_jaxpr/dot_general | solution.py:39
  558.3 13.9 %fusion.43 = (f32[512]{0:T(512)S(1)}, f32[512]{0:T(512)S(1)}, f32[512,4096]{1,0:T(8,128)S(1)}) fusion(f32[4,512,4096]{2,1,0:T(8,128)} %get-tuple-element.295, s32[]{:T(128)} %get-tuple-element.282, f32[64,4096]{1,0:T(8,128)S(1)} %get-tuple-element.297, f32[1,64,512]{2,0,1:T(1,128)S(1)} %constant_dynamic-slice_fusion.11, ...), kind=kOutput, calls=%fused_computation.11.clone.1 | convolution fusion | flops 1629486080 | bytes 17979396 | tf_op jit(solution)/shard_map/while/body/eval_jaxpr/dot_general | solution.py:39
  572.3 10.5 %fusion.44 = f32[4,64,512]{2,1,0:T(8,128)S(1)} fusion(f32[4,64,512]{2,1,0:T(8,128)S(1)} %get-tuple-element.283, s32[]{:T(128)} %get-tuple-element.282, f32[64,4096]{1,0:T(8,128)S(1)} %get-tuple-element.297, f32[1,64,512]{2,0,1:T(1,128)S(1)} %constant_dynamic-slice_fusion.11, f32[512]{0:T(512)S(1)} %get-tuple-element.249, ...), kind=kOutput, calls=%fused_computation.16.clone.1 | convolution fusion | flops 1612775424 | bytes 18091008 | tf_op jit(solution)/shard_map/while/body/eval_jaxpr/dot_general | solution.py:50
  584.9 10.9 %all-reduce = f32[2048]{0:T(1024)S(1)} all-reduce(f32[2048]{0:T(1024)S(1)} %bitcast.120), channel_id=4, replica_groups=mesh['row'=8,'col'=4] {'col'}, use_global_device_ids=true, to_apply=%region_15.16.clone | all-reduce | flops 2048 | bytes 16384
  597.1 38.0 %all-reduce.1 = (f32[]{:T(128)}, f32[]{:T(128)}) all-reduce(f32[]{:T(128)} %get-tuple-element.147, f32[]{:T(128)} %get-tuple-element.156), channel_id=1, replica_groups=mesh['row'=8,'col'=4] {'row','col'}, use_global_device_ids=true, to_apply=%region_17.18 | all-reduce | flops 2 | bytes 16 | tf_op jit(solution)/shard_map/psum | solution.py:103
  (79 shorter events, 92.4 us)
Async XLA Ops:
  8.0 84.2 %copy-start.1 = (bf16[512,1024]{1,0:T(8,128)(2,1)S(1)}, bf16[512,1024]{1,0:T(8,128)(2,1)}, u32[]{:S(2)}) copy-start(bf16[512,1024]{1,0:T(8,128)(2,1)} %param.6) | copy-start | bytes 3145732
  8.0 222.0 %all-reduce.5.cloned.1.call-start = ((), (), s32[]{:S(2)}) async-start(), calls=%async_computation.6 | async-start | bytes 16777216 | tf_op jit(solution)/shard_map/psum | solution.py:13
  8.1 28.5 %collective-permute-start = (bf16[512,1024]{1,0:T(8,128)(2,1)}, bf16[512,1024]{1,0:T(8,128)(2,1)S(1)}, u32[]{:S(2)}, u32[]{:S(2)}) collective-permute-start(bf16[512,1024]{1,0:T(8,128)(2,1)} %param.6), channel_id=1, source_target_pairs={{0,1},{1,2},{2,3},{3,0},{4,5},{5,6},{6,7},{7,4},{8,9},{9,10},{10,1... | collective-permute-start | bytes 3145736 | tf_op jit(solution)/shard_map/ppermute | solution.py:76
  36.5 26.1 %collective-permute-start.1 = (bf16[512,1024]{1,0:T(8,128)(2,1)S(1)}, bf16[512,1024]{1,0:T(8,128)(2,1)S(1)}, u32[]{:S(2)}, u32[]{:S(2)}) collective-permute-start(bf16[512,1024]{1,0:T(8,128)(2,1)S(1)} %collective-permute-done), channel_id=1, source_target_pairs={{0,1},{1,2},{2,3},{3,0},{4,5},{5,6},{6,7},{7,4},{8,9},{9,10},{10,1... | collective-permute-start | bytes 3145736 | tf_op jit(solution)/shard_map/ppermute | solution.py:76
  62.7 25.3 %collective-permute-start.2 = (bf16[512,1024]{1,0:T(8,128)(2,1)S(1)}, bf16[512,1024]{1,0:T(8,128)(2,1)}, u32[]{:S(2)}, u32[]{:S(2)}) collective-permute-start(bf16[512,1024]{1,0:T(8,128)(2,1)S(1)} %collective-permute-done.1), channel_id=1, source_target_pairs={{0,1},{1,2},{2,3},{3,0},{4,5},{5,6},{6,7},{7,4},{8,9},{9,10},{10,1... | collective-permute-start | bytes 3145736 | tf_op jit(solution)/shard_map/ppermute | solution.py:76
  92.3 3.2 copy-start
  100.6 214.5 %all-gather.3.cloned.1.call-start = ((), (), s32[]{:S(2)}) async-start(), calls=%async_computation.2 | async-start | bytes 4325376 | tf_op jit(solution)/shard_map/all_gather | solution.py:90
  101.2 318.1 %reduce-scatter.3.cloned.1.call-start = ((), (), s32[]{:S(2)}) async-start(), calls=%async_computation.3 | async-start | bytes 655360 | tf_op jit(solution)/shard_map/reduce_scatter | solution.py:97
  230.0 19.3 %slice-start = ((s8[8388608]{0:T(1024)(128)(4,1)}), s8[4194304]{0:T(1024)(128)(4,1)S(1)}, s32[]{:S(2)}) async-start(s8[8388608]{0:T(1024)(128)(4,1)} %bitcast.111), calls=%async_computation.7 | async-start | bytes 8388608
  235.4 14.0 %slice-start.1 = ((s8[8388608]{0:T(1024)(128)(4,1)}), s8[4194304]{0:T(1024)(128)(4,1)S(1)}, s32[]{:S(2)}) async-start(s8[8388608]{0:T(1024)(128)(4,1)} %bitcast.111), calls=%async_computation.8 | async-start | bytes 8388608
  397.3 83.8 %all-gather.5.cloned.1.call-start = ((), (), s32[]{:S(2)}) async-start(), calls=%async_computation.4 | async-start | bytes 4325376 | tf_op jit(solution)/shard_map/all_gather | solution.py:90
  420.8 215.6 %reduce-scatter.5.cloned.1.call-start = ((), (), s32[]{:S(2)}) async-start(), calls=%async_computation.5 | async-start | bytes 655360 | tf_op jit(solution)/shard_map/reduce_scatter | solution.py:97
  484.0 99.7 %copy-start.2 = (u32[32]{0:T(128)S(1)}, u32[32]{0:T(128)}, u32[]{:S(2)}) copy-start(u32[32]{0:T(128)} %constant.97) | copy-start | bytes 388
Sparse Core Ops, SparseCore 0:
  100.7 129.2 all-reduce.4
  397.4 21.7 reduce-scatter.2
  583.8 20.1 reduce-scatter.4
Sparse Core Ops, SparseCore 1:
  104.6 76.0 all-gather.2
  420.9 60.1 all-gather.4
